TPU v7x, 256 devices: a whole 4x4x8 slice. The times are simulated.
256 devices in a mesh: gx: 8 (over y, core), gy: 32 (over x, z).
Axes of the slice: x: 4, y: 4, z: 8, core: 2. Of those that a mesh axis runs over, the one named last changes fastest.
Arguments:
- inputs: bfloat16 [32, 64, 128, 128], P(None, 'gx', 'gy'), may hold values from -6 to 6
- cotangent: bfloat16 [32, 64, 128, 128], P(None, 'gx', 'gy'), may hold values from -6 to 6
- kernel: bfloat16 [3, 3, 3, 32, 32], replicated, may hold values from -0.21875 to 0.21875
- channel_bias: float32 [32], replicated, may hold values from -3 to 3
- spectral: bfloat16 [32, 32, 4096], replicated, may hold values from -3 to 3
Outputs:
- outputs: bfloat16 [32, 64, 128, 128], P(None, 'gx', 'gy')
- input_grad: bfloat16 [32, 64, 128, 128], P(None, 'gx', 'gy')
- spectral_grad: float32 [32, 32, 4096], P(None, None, ('gx', 'gy'))
- kernel_grad: float32 [3, 3, 3, 32, 32], replicated
- bias_grad: float32 [32], replicated
All inputs are finite; a program needn't handle non-finite values.
Results may differ from a plain program's by a relative error of at most 0.005.
Values may be sent and summed in bfloat16 or wider, within the bound.
A program may use at most 128 MiB of HBM per device.

v0:
```python
import functools
import math

import jax
import jax.numpy as jnp
import numpy as np
from jax import lax
from jax.experimental import pallas as pl
from jax.experimental.pallas import tpu as pltpu
from jax.sharding import PartitionSpec as P

MESH = pl.DeviceIdType.MESH
MODES = 16
C = 32
BX, BY, NZ = 8, 4, 128
NX, NY = 64, 128
LANES = BY * NZ
WIDE = (BY + 2) * NZ
NEIGHBOURS = [(i, j) for i in (-1, 0, 1) for j in (-1, 0, 1) if (i, j) != (0, 0)]
GRID_SCALE = 1.0 / math.sqrt(NX * NY * NZ)
MODE_SCALE = 1.0 / math.sqrt(MODES**3)
Y_CLASSES = ((1, 6), (6, 10), (10, 14), (14, 16))
KG_ROWS = 32
KG_SHARES = 7
f32, bf16 = jnp.float32, jnp.bfloat16
DOT_NT = (((1,), (1,)), ((), ()))
DOT_TN = (((0,), (0,)), ((), ()))
DOT_NN = (((1,), (0,)), ((), ()))


def basis(cells):
    rows = np.arange(MODES)
    frequency = np.where(rows < MODES // 2, rows, rows - MODES // 2 + 1)
    phase = frequency[:, None] * np.arange(cells)[None, :] % cells
    angles = phase * (2.0 * math.pi / cells)
    return np.where((rows < MODES // 2)[:, None], np.cos(angles), np.sin(angles)).astype(np.float32)


def split(array):
    high = array.astype(jnp.bfloat16)
    low = (array - high.astype(np.float32)).astype(jnp.bfloat16)
    return high, low


def tables():
    phi_x, phi_y, phi_z = basis(NX), basis(NY), basis(NZ)
    high, low = split(phi_z)
    z_analysis = np.concatenate([high, low], 0)
    z_synthesis = np.concatenate([high, high, low], 0)
    lanes = np.repeat(phi_y.reshape(MODES, 32, BY), C, axis=2)
    y_table = lanes.transpose(1, 0, 2)
    x_table = phi_x.T.reshape(-1)
    return z_analysis, z_synthesis, np.ascontiguousarray(y_table), np.ascontiguousarray(x_table)


def dot(a, b, dims):
    return lax.dot_general(a, b, dims, preferred_element_type=f32)


def x_z_synthesise(cell, recv, px_ref, zs_ref):
    values = [recv[p].astype(f32) for p in range(MODES)]
    planes = []
    for i in range(BX):
        total = px_ref[(cell + i) * 16] * values[0]
        for p in range(1, MODES):
            total = total + px_ref[(cell + i) * 16 + p] * values[p]
        planes.append(total)
    total = jnp.concatenate(planes, axis=1)
    high = total.astype(bf16)
    low = (total - high.astype(f32)).astype(bf16)
    return dot(jnp.concatenate([high, low, high], axis=0), zs_ref[...], DOT_TN)


def kernel(
    x_hbm, ct_hbm, spec_hbm, w_hbm, bias_hbm, za_hbm, zs_hbm, py_hbm, px_hbm,
    out_ref, ig_ref, sg_ref, kr3,
    w_raw, bias_row, za_ref, zs_ref, py_ref, px_ref, wf_ref, wb_ref, bias_ref,
    xin, ctin, spec, flat, ct, acc, stk, dstk, dx, tbuf,
    sx, rx, sy, ry, sz, rz, ct_modes, coefs, mixed,
    sxb, rxb, syb, ryb, szb, rzb,
    ks1, kr1, ks2, kr2, ks3,
    oflat, flat2, by_input,
    ready, dma_sem, halo_s, halo_r, xs, xr, ys, yr, zs, zr, k1s, k1r, k2s, k2r, k3s, k3r,
):
    a, b = lax.axis_index("gx"), lax.axis_index("gy")
    h, q = b // 16, lax.rem(b, 16)
    g = 2 * a + h
    partner = (3 - b // 8) * 8 + lax.rem(b, 8)

    load_x = pltpu.make_async_copy(x_hbm, xin, dma_sem.at[0])
    load_x.start()

    def group_x(k):
        rank, other, core = k // 4, lax.rem(k // 2, 2), lax.rem(k, 2)
        steps = jnp.where(rank == 1, 3, jnp.where(rank == 0, 0, rank - 1))
        ta = 2 * lax.rem(a // 2 + steps, 4) + lax.rem(a + core, 2)
        th = lax.rem(h + other, 2)
        return 2 * ta + th, (ta, jnp.where(other == 0, b, partner))

    def group_y(k):
        rank, other = k // 2, lax.rem(k, 2)
        steps = jnp.where(lax.rem(rank, 2) == 1, (rank + 1) // 2, 8 - rank // 2)
        t = 8 * lax.rem(q // 8 + other, 2) + lax.rem(lax.rem(q, 8) + steps, 8)
        return t, (a, t + 16 * h)

    def each(members, action, count=15):
        def step(n, carry):
            action(count - n, *members(count - n))
            return carry

        lax.fori_loop(0, count, step, 0, unroll=True)

    def there(da, db):
        ok = None
        if da == 1:
            ok = a < 7
        if da == -1:
            ok = a > 0
        if db == 1:
            ok = (b < 31) if ok is None else ok & (b < 31)
        if db == -1:
            ok = (b > 0) if ok is None else ok & (b > 0)
        return ok

    barrier = pltpu.get_barrier_semaphore()

    def greet(k, t, peer):
        pl.semaphore_signal(barrier, inc=1, device_id=peer, device_id_type=MESH)

    each(group_x, greet)
    each(group_y, greet, 9)
    awaited = 24
    for da, db in NEIGHBOURS:
        if db == 0:
            continue

        @pl.when(there(da, db))
        def _():
            pl.semaphore_signal(barrier, inc=1, device_id=(a + da, b + db), device_id_type=MESH)

        awaited = awaited + jnp.where(there(da, db), 1, 0)

    load_ct = pltpu.make_async_copy(ct_hbm, ctin, dma_sem.at[1])
    load_spec = pltpu.make_async_copy(
        spec_hbm.at[:, :, pl.ds(pl.multiple_of(g * 256, 256), 256)], spec, dma_sem.at[2]
    )
    small = [
        pltpu.make_async_copy(src, dst, dma_sem.at[5 + n])
        for n, (src, dst) in enumerate(
            ((za_hbm, za_ref), (px_hbm, px_ref), (w_hbm, w_raw), (bias_hbm, bias_row), (zs_hbm, zs_ref), (py_hbm, py_ref))
        )
    ]
    for load in small:
        load.start()
    load_ct.start()
    load_spec.start()

    def x_copy(t, peer, src, buf, ssem, rsem):
        return pltpu.make_async_remote_copy(
            src_ref=src, dst_ref=buf.at[g], send_sem=ssem, recv_sem=rsem,
            device_id=peer, device_id_type=MESH,
        )

    def y_copy(t, peer, src, buf, ssem, rsem):
        return pltpu.make_async_remote_copy(
            src_ref=src, dst_ref=buf.at[q], send_sem=ssem, recv_sem=rsem,
            device_id=peer, device_id_type=MESH,
        )

    def all_of(buf, count, ssem, rsem):
        return pltpu.make_async_remote_copy(
            src_ref=buf.at[pl.ds(0, count)], dst_ref=buf.at[pl.ds(0, count)], send_sem=ssem, recv_sem=rsem,
            device_id=group_y(1)[1], device_id_type=MESH,
        )

    def halo_copy(index, field, n, da, db):
        sx_ = pl.ds(8, 1) if da == 1 else pl.ds(1, 1) if da == -1 else pl.ds(1, 8)
        dx_ = pl.ds(0, 1) if da == 1 else pl.ds(9, 1) if da == -1 else pl.ds(1, 8)
        sl = pl.ds(512, 128) if db == 1 else pl.ds(128, 128) if db == -1 else pl.ds(128, 512)
        dl = pl.ds(0, 128) if db == 1 else pl.ds(640, 128) if db == -1 else pl.ds(128, 512)
        return pltpu.make_async_remote_copy(
            src_ref=field.at[sx_, pl.ds(32, 32), sl], dst_ref=field.at[dx_, pl.ds(32, 32), dl],
            send_sem=halo_s.at[n, index], recv_sem=halo_r.at[n, index],
            device_id=(a + da, b + db), device_id_type=MESH,
        )

    def halo_start(field, n):
        for index, (da, db) in enumerate(NEIGHBOURS):

            @pl.when(there(da, db))
            def _():
                halo_copy(index, field, n, da, db).start()

    def halo_wait_recv(field, n):
        for index, (da, db) in enumerate(NEIGHBOURS):

            @pl.when(there(-da, -db))
            def _():
                halo_copy(index, field, n, da, db).wait_recv()

    def halo_wait_send(field, n):
        for index, (da, db) in enumerate(NEIGHBOURS):

            @pl.when(there(da, db))
            def _():
                halo_copy(index, field, n, da, db).wait_send()

    def zero_rim(field):
        @pl.when(a == 0)
        def _():
            field[0, 32:64, :] = jnp.zeros((C, WIDE), bf16)

        @pl.when(a == 7)
        def _():
            field[9, 32:64, :] = jnp.zeros((C, WIDE), bf16)

        @pl.when(b == 0)
        def _():
            for i in range(10):
                field[i, 32:64, 0:128] = jnp.zeros((C, NZ), bf16)

        @pl.when(b == 31)
        def _():
            for i in range(10):
                field[i, 32:64, 640:768] = jnp.zeros((C, NZ), bf16)

    def z_analyse(i, tiles):
        rows = jnp.concatenate(tiles, axis=0)
        both = dot(za_ref[...], rows, DOT_NT)
        tbuf[i] = both[:16] + both[16:]

    def x_partials(buf):
        rows = [tbuf[i] for i in range(BX)]

        def step(p, carry):
            total = px_ref[(a * 8) * 16 + p] * rows[0]
            for i in range(1, BX):
                total = total + px_ref[(a * 8 + i) * 16 + p] * rows[i]
            buf[p] = total
            return carry

        lax.fori_loop(0, 16, step, 0, unroll=4)

    def y_blocks(recv, send):
        for half in range(2):
            total = recv[half]
            for i in range(1, 8):
                total = total + recv[2 * i + half]
            send[half] = total.astype(bf16)

    def block_of(member, half):
        return 16 * half + jnp.where(h == half, member, lax.rem(member + 8, 16))

    def y_analyse(recv, n):
        def step(k, carry):
            result = list(carry)
            block = group_y(k)[0]
            for half in range(2):
                value = recv[block, half].astype(f32)
                place = block_of(block, half)
                for m in range(MODES):
                    result[m] = result[m] + value * py_ref[place, pl.ds(m, 1), :]
            return tuple(result)

        result = step(0, tuple(jnp.zeros((16, 128), f32) for _ in range(MODES)))
        for near, (low, high) in enumerate(Y_CLASSES):
            all_of(recv, high - low, ys.at[n], yr.at[n, near]).wait_recv()
            result = lax.fori_loop(low, high, step, result, unroll=True)
        return result

    def y_class(k):
        return jnp.where(k < 6, 0, jnp.where(k < 10, 1, jnp.where(k < 14, 2, 3)))

    def to_columns(parts, scale):
        wide = jnp.transpose(jnp.concatenate(parts, axis=0))
        return (wide[0:32] + wide[32:64] + wide[64:96] + wide[96:128]) * scale

    def y_synthesise(modes, scale, send):
        tall = jnp.transpose(jnp.concatenate([modes * scale] * 4, axis=0))
        for half in range(2):
            place = block_of(q, half)
            total = py_ref[place, pl.ds(0, 1), :] * tall[0:16]
            for m in range(1, MODES):
                total = total + py_ref[place, pl.ds(m, 1), :] * tall[16 * m : 16 * m + 16]
            send[half] = total.astype(send.dtype)

    lane = lax.broadcasted_iota(jnp.int32, (C, NZ), 1)

    def shift_rows(field, ones):
        def step(i, carry):
            for y in range(BY + 2):
                cells = slice(y * NZ, (y + 1) * NZ)
                value = field[i, 32:64, cells].astype(f32)
                before = jnp.where(lane == 0, 0.0, pltpu.roll(value, 1, 1))
                after = jnp.where(lane == NZ - 1, 0.0, pltpu.roll(value, NZ - 1, 1))
                field[i, 0:32, cells] = before.astype(bf16)
                field[i, 64:96, cells] = after.astype(bf16)
            return carry

        lax.fori_loop(0, 10, step, 0, unroll=2)

    def fill_ones(field):
        def step(i, carry):
            field[i, 96:128, :] = jnp.ones((32, WIDE), bf16)
            return carry

        lax.fori_loop(0, 10, step, 0)

    def convolve(field, weights, shift=None):
        def step(i, carry):
            total = None
            for d in range(3):
                for e in range(3):
                    tap = (d * 3 + e) * 128
                    part = dot(
                        weights[:, tap : tap + 128], field[i + d, :, e * NZ : e * NZ + LANES], DOT_NN
                    )
                    total = part if total is None else total + part
            acc[i] = total if shift is None else total + shift
            return carry

        lax.fori_loop(0, BX, step, 0, unroll=2)

    def unflatten(source, write):
        def step(c, carry):
            flat[pl.ds(pl.multiple_of(c * 32, 32), 32), :] = source[c].astype(f32)
            return carry

        lax.fori_loop(0, C, step, 0, unroll=8)

        def step2(i, carry):
            tiles = [flat[pl.ds(i * BY + y, C, stride=32), :] for y in range(BY)]
            write(i, tiles)
            return carry

        lax.fori_loop(0, BX, step2, 0, unroll=4)

    def flatten(source, target):
        def step(c, carry):
            target[c] = source[pl.ds(pl.multiple_of(c * 32, 32), 32), :].astype(bf16)
            return carry

        lax.fori_loop(0, C, step, 0, unroll=8)

    def prepare_weights():
        row = lax.broadcasted_iota(jnp.int32, (C, 128), 0)
        column = lax.broadcasted_iota(jnp.int32, (C, 128), 1)
        place = [jnp.where(column == row + 32 * f, 1.0, 0.0).astype(bf16) for f in range(3)]
        for tap in range(9):
            total, back_total = None, None
            for f in range(3):
                part = dot(w_raw[tap * 3 + f], place[f], DOT_NN)
                total = part if total is None else total + part
                part = dot(w_raw[(8 - tap) * 3 + 2 - f], place[f], DOT_TN)
                back_total = part if back_total is None else back_total + part
            wf_ref[:, tap * 128 : tap * 128 + 128] = total.astype(bf16)
            wb_ref[:, tap * 128 : tap * 128 + 128] = back_total.astype(bf16)
        spread = jnp.where(column[:, :C] == row[:, :C], jnp.broadcast_to(bias_row[...], (C, C)), 0.0)
        bias_ref[...] = jnp.broadcast_to(jnp.sum(spread, axis=1, keepdims=True), (C, 128))

    load_x.wait()
    small[0].wait()
    small[1].wait()

    def write_x(i, tiles):
        tiles = [t.astype(bf16) for t in tiles]
        for y in range(BY):
            stk[i + 1, 32:64, (y + 1) * NZ : (y + 2) * NZ] = tiles[y]
        z_analyse(i, tiles)

    unflatten(xin, write_x)
    x_partials(sx)
    pl.semaphore_wait(barrier, awaited)
    for k in (6, 8):
        pl.semaphore_signal(ready, inc=1, device_id=group_y(k)[1], device_id_type=MESH)
    each(group_x, lambda k, t, peer: x_copy(t, peer, sx.at[t], rx, xs.at[0], xr.at[0]).start())
    rx[g] = sx[g]
    halo_start(stk, 0)

    zero_rim(stk)
    fill_ones(stk)
    for load in small[2:]:
        load.wait()
    prepare_weights()
    load_ct.wait()

    def write_ct(i, tiles):
        for y in range(BY):
            ct[i, :, y * NZ : (y + 1) * NZ] = tiles[y]

    unflatten(ctin, write_ct)
    for i in (0, 1, 10, 11):
        dx[i] = jnp.zeros((C, LANES), bf16)

    all_of(rx, 15, xs.at[0], xr.at[0]).wait_recv()
    y_blocks(rx, sy)
    pl.semaphore_wait(ready, 2)
    each(group_y, lambda k, t, peer: y_copy(t, peer, sy, ry, ys.at[0], yr.at[0, y_class(k)]).start())
    ry[q] = sy[...]

    halo_wait_recv(stk, 0)
    shift_rows(stk, True)
    convolve(stk, wf_ref, jnp.concatenate([bias_ref[...]] * BY, axis=1))
    load_spec.wait()

    def widen(o, carry):
        for n in range(2):
            flat2[n, pl.ds(pl.multiple_of(o * 32, 32), 32), :] = spec[o, :, 128 * n : 128 * n + 128].astype(f32)
        return carry

    lax.fori_loop(0, C, widen, 0, unroll=4)

    def gather(c, carry):
        for n in range(2):
            by_input[c, :, 128 * n : 128 * n + 128] = flat2[n, pl.ds(c, C, stride=32), :]
        return carry

    lax.fori_loop(0, C, gather, 0, unroll=4)

    parts = y_analyse(ry, 0)
    for m in range(MODES):
        ct_modes[0, m] = parts[m]
    coefs[...] = to_columns(parts, GRID_SCALE)

    def mix(c, carry):
        return carry + by_input[c] * coefs[pl.ds(c, 1), :]

    y_synthesise(lax.fori_loop(0, C, mix, jnp.zeros((C, 256), f32), unroll=4), MODE_SCALE, sz)
    each(group_x, lambda k, t, peer: x_copy(t, peer, sz.at[lax.rem(t, 2)], rz, zs.at[0], zr.at[0]).start())
    rz[g] = sz[h]
    all_of(rz, 15, zs.at[0], zr.at[0]).wait_recv()

    root = math.sqrt(2.0 / math.pi)

    modes_all = x_z_synthesise(a * 8, rz, px_ref, zs_ref)

    def point(i):
        modes = modes_all[128 * i : 128 * i + 128]
        tiles = []
        for y in range(BY):
            cells = slice(y * NZ, (y + 1) * NZ)
            v = acc[i, :, cells] + modes[y * C : (y + 1) * C]
            square = v * v
            t = jnp.tanh(v * (square * (0.044715 * root) + root))
            half = 0.5 * t + 0.5
            slope = half * ((v * (square * (3 * 0.044715 * root) + root)) * (1.0 - t) + 1.0)
            acc[i, :, cells] = v * half
            delta = (ct[i, :, cells] * slope).astype(bf16)
            dstk[i + 1, 32:64, (y + 1) * NZ : (y + 2) * NZ] = delta
            dx[i + 2, :, cells] = delta
            tiles.append(delta)
        z_analyse(i, tiles)

    for i in range(BX):
        point(i)

    x_partials(sxb)
    each(group_x, lambda k, t, peer: x_copy(t, peer, sxb.at[t], rxb, xs.at[1], xr.at[1]).start())
    rxb[g] = sxb[g]

    def planes(cut):
        return jnp.concatenate([cut(i) for i in range(10)], axis=1)

    idle = jnp.zeros((C, LANES), bf16)
    shifted = [planes(lambda i, d=d: dx[i + 2 - d]) for d in range(3)] + [planes(lambda i: idle)]
    windows = [planes(lambda i, e=e: stk[i, : 112 if e == 1 else 96, e * NZ : e * NZ + LANES]) for e in range(3)]
    kgt = dot(jnp.concatenate(windows, axis=0), jnp.concatenate(shifted, axis=0), DOT_NT)
    empty = jnp.zeros((32, 128), f32)
    kgt = [
        jnp.concatenate([kgt[0:96], empty], axis=0),
        jnp.concatenate([kgt[96:208], empty[:16]], axis=0),
        jnp.concatenate([kgt[208:304], empty], axis=0),
    ]
    columns = [jnp.transpose(kgt[e]) for e in range(3)]
    kgp = [columns[e][32 * d : 32 * d + 32] for e in range(3) for d in range(3)]

    for n in range(7):
        block = kgp[n]
        if n < 6:
            block = jnp.where(lane >= 96, pltpu.roll(kgp[7 + n // 3], 96 - 32 * (n % 3), 1), block)
        else:
            block = jnp.where(lane >= 96, kgp[4], block)
        ks1[n] = block.astype(bf16)
    def share_of(t):
        return t // 2 + lax.rem(t, 2), (lax.rem(t // 2, 2) == 0) & (t // 2 + lax.rem(t, 2) < KG_SHARES)

    share, holds = share_of(g)

    def k1_start(k, t, peer):
        target, takes = share_of(t)

        @pl.when(takes)
        def _():
            x_copy(t, peer, ks1.at[target], kr1, k1s, k1r).start()

    each(group_x, k1_start)

    halo_start(dstk, 1)

    zero_rim(dstk)
    fill_ones(dstk)
    def spread(i, carry):
        for y in range(BY):
            oflat[pl.ds(i * BY + y, C, stride=32), :] = acc[i, :, y * NZ : (y + 1) * NZ]
        return carry

    lax.fori_loop(0, BX, spread, 0, unroll=4)
    flatten(oflat, out_ref)

    all_of(rxb, 15, xs.at[1], xr.at[1]).wait_recv()
    y_blocks(rxb, syb)
    each(group_y, lambda k, t, peer: y_copy(t, peer, syb, ryb, ys.at[1], yr.at[1, y_class(k)]).start())
    ryb[q] = syb[...]

    @pl.when(holds)
    def _():
        all_of(kr1, 15, k1s, k1r).wait_recv()
        kr1[g] = ks1[share]
        total = kr1[0].astype(f32)
        for i in range(1, 16):
            total = total + kr1[i].astype(f32)
        ks2[...] = total.astype(bf16)
        kr2[q] = total.astype(bf16)
        each(group_y, lambda k, t, peer: y_copy(t, peer, ks2, kr2, k2s, k2r).start())

    halo_wait_recv(dstk, 1)
    shift_rows(dstk, False)
    convolve(dstk, wb_ref)

    parts = y_analyse(ryb, 1)
    for m in range(MODES):
        ct_modes[1, m] = parts[m]
    mixed[...] = to_columns(parts, MODE_SCALE)

    def mix_back(o, carry):
        return carry + spec[o].astype(f32) * mixed[pl.ds(o, 1), :]

    back = lax.fori_loop(0, C, mix_back, jnp.zeros((C, 256), f32), unroll=4)
    y_synthesise(back, GRID_SCALE, szb)
    each(group_x, lambda k, t, peer: x_copy(t, peer, szb.at[lax.rem(t, 2)], rzb, zs.at[1], zr.at[1]).start())
    rzb[g] = szb[h]

    def share_copy(peer):
        return pltpu.make_async_remote_copy(
            src_ref=ks3, dst_ref=kr3.at[share], send_sem=k3s, recv_sem=k3r, device_id=peer, device_id_type=MESH
        )

    @pl.when(holds)
    def _():
        all_of(kr2, 15, k2s, k2r).wait_recv()
        total = kr2[0].astype(f32)
        for i in range(1, 16):
            total = total + kr2[i].astype(f32)
        total = total * GRID_SCALE
        ks3[...] = total.astype(bf16)
        kr3[share] = total.astype(bf16)
        each(group_x, lambda k, t, peer: share_copy(peer).start())

    coef_rows = ct_modes[0, q]
    coef_rows = coef_rows + pltpu.roll(coef_rows, 64, 1)
    coef_rows = (coef_rows + pltpu.roll(coef_rows, 32, 1)) * GRID_SCALE
    wide = jnp.transpose(ct_modes[1, q])
    back_columns = jnp.transpose(wide[0:32] + wide[32:64] + wide[64:96] + wide[96:128]) * MODE_SCALE
    for o in range(C):
        sg_ref[o] = (coef_rows * back_columns[:, o : o + 1])[:, 0:32]

    all_of(rzb, 15, zs.at[1], zr.at[1]).wait_recv()
    modes_all = x_z_synthesise(a * 8, rzb, px_ref, zs_ref)

    def last(i):
        modes = modes_all[128 * i : 128 * i + 128]
        for y in range(BY):
            cells = slice(y * NZ, (y + 1) * NZ)
            oflat[pl.ds(i * BY + y, C, stride=32), :] = acc[i, :, cells] + modes[y * C : (y + 1) * C]

    for i in range(BX):
        last(i)
    flatten(oflat, ig_ref)

    for n in range(2):
        all_of((rx, rxb)[n], 15, xs.at[n], xr.at[n]).wait_send()
        all_of((rz, rzb)[n], 15, zs.at[n], zr.at[n]).wait_send()
        all_of((ry, ryb)[n], 15, ys.at[n], yr.at[n, 0]).wait_send()
    halo_wait_send(stk, 0)
    halo_wait_send(dstk, 1)
    def in_shares(has, has_not):
        pl.when(holds)(has)
        pl.when(jnp.logical_not(holds))(has_not)

    in_shares(
        lambda: all_of(kr1, KG_SHARES - 1, k1s, k1r).wait_send(),
        lambda: all_of(kr1, KG_SHARES, k1s, k1r).wait_send(),
    )

    @pl.when(holds)
    def _():
        all_of(kr2, 15, k2s, k2r).wait_send()
        all_of(kr1, 15, k3s, k3r).wait_send()

    in_shares(
        lambda: all_of(kr3, KG_SHARES - 1, k3s, k3r).wait_recv(),
        lambda: all_of(kr3, KG_SHARES, k3s, k3r).wait_recv(),
    )


def finish(kr, ig, out, sg, out_hbm, ig_hbm, sg_hbm, kg_hbm, bg_hbm, kg, bg, store_sem):
    pairs = ((ig, ig_hbm), (out, out_hbm), (sg, sg_hbm), (bg, bg_hbm), (kg, kg_hbm))
    stores = [pltpu.make_async_copy(src, dst, store_sem.at[n]) for n, (src, dst) in enumerate(pairs)]
    for store in stores[:3]:
        store.start()
    blocks = [kr[n].astype(f32) for n in range(KG_SHARES)]
    bg[...] = jnp.transpose(blocks[6])[96:97, :]
    stores[3].start()
    for d in range(3):
        for e in range(3):
            for f in range(3):
                n, offset = e * 3 + d, 32 * f
                if n >= 7:
                    n, offset = (n - 7) * 3 + f, 96
                moved = blocks[n] if offset == 0 else pltpu.roll(blocks[n], 128 - offset, 1)
                kg[(d * 3 + e) * 3 + f] = moved[:, 0:32]
    stores[4].start()
    for store in stores:
        store.wait()


def layer(inputs, cotangent, weights, channel_bias, spectral):
    z_analysis, z_synthesis, y_table, x_table = tables()
    x = inputs.reshape(C, BX * BY, NZ)
    ct = cotangent.reshape(C, BX * BY, NZ)
    any_space = pl.BlockSpec(memory_space=pl.ANY)
    vmem = pl.BlockSpec(memory_space=pltpu.VMEM)
    dma = pltpu.SemaphoreType.DMA
    V = pltpu.VMEM
    mode_bufs = [
        V((16, 16, 128), f32), V((16, 16, 128), f32),
        V((2, 16, 128), bf16), V((16, 2, 16, 128), bf16),
        V((2, 16, 128), bf16), V((16, 16, 128), bf16),
    ]
    block = (C, BX * BY, NZ)
    operands = (
        x, ct, spectral, weights.reshape(27, C, C), channel_bias.reshape(1, C),
        z_analysis, z_synthesis, y_table, x_table,
    )
    results = pl.pallas_call(
        kernel,
        out_shape=(V(block, bf16), V(block, bf16), V((C, 16, C), f32), V((KG_SHARES, KG_ROWS, 128), bf16)),
        in_specs=[pl.BlockSpec(memory_space=pltpu.HBM)] * 9,
        out_specs=(vmem,) * 4,
        scratch_shapes=[
            V((27, C, C), bf16), V((1, C), f32), V((32, 128), bf16), V((48, 128), bf16),
            V((32, MODES, 128), f32), pltpu.SMEM((NX * MODES,), f32),
            V((C, 1152), bf16), V((C, 1152), bf16), V((C, 128), f32),
            V((C, 32, NZ), bf16), V((C, 32, NZ), bf16), V((C, C, 256), bf16),
            V((C * 32, NZ), f32), V((BX, C, LANES), f32), V((BX, C, LANES), f32),
            V((10, 128, WIDE), bf16), V((10, 128, WIDE), bf16), V((12, C, LANES), bf16),
            V((BX, 16, 128), f32),
            *mode_bufs,
            V((2, MODES, 16, 128), f32), V((C, 256), f32), V((C, 256), f32),

            *mode_bufs,
            V((KG_SHARES, KG_ROWS, 128), bf16), V((16, KG_ROWS, 128), bf16),
            V((KG_ROWS, 128), bf16), V((16, KG_ROWS, 128), bf16),
            V((KG_ROWS, 128), bf16),
            V((C * 32, NZ), f32), V((2, C * C, 128), f32), V((C, C, 256), f32),
            pltpu.SemaphoreType.REGULAR, dma((11,)), dma((2, 8)), dma((2, 8)),
            *[dma((2,))] * 3, dma((2, 4)), *[dma((2,))] * 2,
            *[dma] * 6,
        ],
        compiler_params=pltpu.CompilerParams(
            collective_id=0, has_side_effects=True, vmem_limit_bytes=40 * 2**20
        ),
        cost_estimate=pl.CostEstimate(flops=700_000_000, bytes_accessed=4_000_000, transcendentals=131072),
    )(*[pltpu.with_memory_space_constraint(jnp.asarray(operand), pltpu.HBM) for operand in operands])
    outputs, input_grad, spectral_grad, shares = [
        pltpu.with_memory_space_constraint(result, pltpu.VMEM) for result in results
    ]
    outputs, input_grad, spectral_grad, kernel_grad, bias_grad = pl.pallas_call(
        finish,
        out_shape=(
            jax.ShapeDtypeStruct(block, bf16),
            jax.ShapeDtypeStruct(block, bf16),
            jax.ShapeDtypeStruct((C, 16, C), f32),
            jax.ShapeDtypeStruct((27, C, C), f32),
            jax.ShapeDtypeStruct((1, C), f32),
        ),
        in_specs=[vmem] * 4,
        out_specs=(any_space,) * 5,
        scratch_shapes=[
            V((27, C, C), f32), V((1, C), f32), dma((5,)),
        ],
        compiler_params=pltpu.CompilerParams(vmem_limit_bytes=16 * 2**20),
    )(shares, input_grad, outputs, spectral_grad)
    field = (C, BX, BY, NZ)
    return (
        outputs.reshape(field), input_grad.reshape(field), spectral_grad.transpose(0, 2, 1),
        kernel_grad.reshape(3, 3, 3, C, C), bias_grad.reshape(C),
    )


def solution(mesh):
    placed = (P(None, "gx", "gy", None), P(None, "gx", "gy", None), P(), P(), P())
    return jax.shard_map(
        layer,
        mesh=mesh,
        in_specs=placed,
        out_specs=(
            P(None, "gx", "gy", None),
            P(None, "gx", "gy", None),
            P(None, None, ("gx", "gy")),
            P(),
            P(),
        ),
        check_vma=False,
    )
```

profile of v0, /device:TPU:1, one launch (start us, length us, event | category | flops | bytes accessed | tf_op | source)
XLA Modules:
  0.0 44.3 jit_solution(15245485147196754799)
XLA Ops:
  0.6 42.6 %shard_map.128 = (bf16[32,32,128]{2,1,0:T(8,128)(2,1)S(1)}, bf16[32,32,128]{2,1,0:T(8,128)(2,1)S(1)}, f32[32,16,32]{2,1,0:T(8,128)S(1)}, bf16[7,32,128]{2,1,0:T(8,128)(2,1)S(1)}) custom-call(bf16[32,32,128]{2,1,0:T(8,128)(2,1)} %bitcast.9, bf16[32,32,128]{2,1,0:T(8,128)(2,1)} %bitcast.10, bf16[32,32,4096]{2,1,0:T(8,128)(2,1)} %spec_hbm.1, ...), custom_call_target="tpu_custom_call" | custom-call | flops 700000000 | bytes 4000000 | tf_op jit(solution)/shard_map/pallas_call | solution.py:645
  43.2 1.1 %shard_map.129 = (bf16[32,32,128]{2,1,0:T(8,128)(2,1)}, bf16[32,32,128]{2,1,0:T(8,128)(2,1)}, f32[32,16,32]{2,1,0:T(8,128)}, f32[27,32,32]{2,1,0:T(8,128)}, f32[1,32]{1,0:T(1,128)}) custom-call(bf16[7,32,128]{2,1,0:T(8,128)(2,1)S(1)} %get-tuple-element.14.kr, bf16[32,32,128]{2,1,0:T(8,128)(2,1)S(1)} %get-tuple-element.15.ig, ...), custom_call_target="tpu_custom_call" | custom-call | tf_op jit(solution)/shard_map/pallas_call | solution.py:678
where the time goes:
time: 44.4 us; the launch traced here: 44.3 us
  Pallas kernels  43.7 us (98%)
  between operations  0.64 us (1%)
    pallas_call x1, Pallas kernels, layer(): pl.pallas_call(kernel, out_shape=(V(block, bf16), V(block, bf16), V((C, 1...  42.6 us
    pallas_call x1, Pallas kernels, layer(): pl.pallas_call(finish, out_shape=(jax.ShapeDtypeStruct(block, bf16), jax....  1.07 us

commit v1 on v0

--- a/solution.py
+++ b/solution.py
@@ -49,8 +49,13 @@
     z_synthesis = np.concatenate([high, high, low], 0)
     lanes = np.repeat(phi_y.reshape(MODES, 32, BY), C, axis=2)
     y_table = lanes.transpose(1, 0, 2)
+    y_table_back = y_table.reshape(32, MODES, BY, C).transpose(0, 1, 3, 2).reshape(32, MODES, BY * C)
     x_table = phi_x.T.reshape(-1)
-    return z_analysis, z_synthesis, np.ascontiguousarray(y_table), np.ascontiguousarray(x_table)
+    y_scale = np.exp2(np.arange(NY) * 0.6180339887 % 1.0).reshape(32, BY)
+    x_scale = np.exp2(np.arange(8 * BY) * 0.6180339887 % 1.0).reshape(8, BY)
+    scales = np.repeat(np.concatenate([y_scale, x_scale, 1.0 / x_scale]), C, axis=1).astype(np.float32)
+    y_analysis = (y_table / np.repeat(y_scale, C, axis=1)[:, None, :]).astype(np.float32)
+    return z_analysis, z_synthesis, np.ascontiguousarray(y_table), np.ascontiguousarray(y_table_back), np.ascontiguousarray(x_table), scales, y_analysis
 
 
 def dot(a, b, dims):
@@ -72,9 +77,9 @@
 
 
 def kernel(
-    x_hbm, ct_hbm, spec_hbm, w_hbm, bias_hbm, za_hbm, zs_hbm, py_hbm, px_hbm,
+    x_hbm, ct_hbm, spec_hbm, w_hbm, bias_hbm, za_hbm, zs_hbm, py_hbm, px_hbm, pb_hbm, sc_hbm, pa_hbm,
     out_ref, ig_ref, sg_ref, kr3,
-    w_raw, bias_row, za_ref, zs_ref, py_ref, px_ref, wf_ref, wb_ref, bias_ref,
+    w_raw, bias_row, za_ref, zs_ref, py_ref, px_ref, pb_ref, sc_ref, pa_ref, wide_ref, wf_ref, wb_ref, bias_ref,
     xin, ctin, spec, flat, ct, acc, stk, dstk, dx, tbuf,
     sx, rx, sy, ry, sz, rz, ct_modes, coefs, mixed,
     sxb, rxb, syb, ryb, szb, rzb,
@@ -147,7 +152,7 @@
     small = [
         pltpu.make_async_copy(src, dst, dma_sem.at[5 + n])
         for n, (src, dst) in enumerate(
-            ((za_hbm, za_ref), (px_hbm, px_ref), (w_hbm, w_raw), (bias_hbm, bias_row), (zs_hbm, zs_ref), (py_hbm, py_ref))
+            ((za_hbm, za_ref), (px_hbm, px_ref), (sc_hbm, sc_ref), (pa_hbm, pa_ref), (w_hbm, w_raw), (bias_hbm, bias_row), (zs_hbm, zs_ref), (py_hbm, py_ref), (pb_hbm, pb_ref))
         )
     ]
     for load in small:
@@ -236,17 +241,17 @@
             total = px_ref[(a * 8) * 16 + p] * rows[0]
             for i in range(1, BX):
                 total = total + px_ref[(a * 8 + i) * 16 + p] * rows[i]
-            buf[p] = total
+            buf[p] = (total * sc_ref[pl.ds(32 + a, 1), :]).astype(bf16)
             return carry
 
         lax.fori_loop(0, 16, step, 0, unroll=4)
 
     def y_blocks(recv, send):
         for half in range(2):
-            total = recv[half]
+            total = recv[half].astype(f32) * sc_ref[40:41, :]
             for i in range(1, 8):
-                total = total + recv[2 * i + half]
-            send[half] = total.astype(bf16)
+                total = total + recv[2 * i + half].astype(f32) * sc_ref[40 + i : 41 + i, :]
+            send[half] = (total * sc_ref[pl.ds(block_of(q, half), 1), :]).astype(bf16)
 
     def block_of(member, half):
         return 16 * half + jnp.where(h == half, member, lax.rem(member + 8, 16))
@@ -259,7 +264,7 @@
                 value = recv[block, half].astype(f32)
                 place = block_of(block, half)
                 for m in range(MODES):
-                    result[m] = result[m] + value * py_ref[place, pl.ds(m, 1), :]
+                    result[m] = result[m] + value * pa_ref[place, pl.ds(m, 1), :]
             return tuple(result)
 
         result = step(0, tuple(jnp.zeros((16, 128), f32) for _ in range(MODES)))
@@ -276,12 +281,21 @@
         return (wide[0:32] + wide[32:64] + wide[64:96] + wide[96:128]) * scale
 
     def y_synthesise(modes, scale, send):
-        tall = jnp.transpose(jnp.concatenate([modes * scale] * 4, axis=0))
+        y_project(jnp.transpose(jnp.concatenate([modes * scale] * 4, axis=0)), py_ref, send)
+
+    def y_synthesise_back(modes, scale, send):
+        for n in range(2):
+            for j in range(BY):
+                wide_ref[n, pl.ds(j, C, stride=BY), :] = modes[:, 128 * n : 128 * n + 128] * scale
+        tall = jnp.concatenate([jnp.transpose(wide_ref[n]) for n in range(2)], axis=0)
+        y_project(tall, pb_ref, send)
+
+    def y_project(tall, table, send):
         for half in range(2):
             place = block_of(q, half)
-            total = py_ref[place, pl.ds(0, 1), :] * tall[0:16]
+            total = table[place, pl.ds(0, 1), :] * tall[0:16]
             for m in range(1, MODES):
-                total = total + py_ref[place, pl.ds(m, 1), :] * tall[16 * m : 16 * m + 16]
+                total = total + table[place, pl.ds(m, 1), :] * tall[16 * m : 16 * m + 16]
             send[half] = total.astype(send.dtype)
 
     lane = lax.broadcasted_iota(jnp.int32, (C, NZ), 1)
@@ -361,6 +375,7 @@
     load_x.wait()
     small[0].wait()
     small[1].wait()
+    small[2].wait()
 
     def write_x(i, tiles):
         tiles = [t.astype(bf16) for t in tiles]
@@ -379,7 +394,7 @@
 
     zero_rim(stk)
     fill_ones(stk)
-    for load in small[2:]:
+    for load in small[3:]:
         load.wait()
     prepare_weights()
     load_ct.wait()
@@ -536,7 +551,7 @@
         return carry + spec[o].astype(f32) * mixed[pl.ds(o, 1), :]
 
     back = lax.fori_loop(0, C, mix_back, jnp.zeros((C, 256), f32), unroll=4)
-    y_synthesise(back, GRID_SCALE, szb)
+    y_synthesise_back(back, GRID_SCALE, szb)
     each(group_x, lambda k, t, peer: x_copy(t, peer, szb.at[lax.rem(t, 2)], rzb, zs.at[1], zr.at[1]).start())
     rzb[g] = szb[h]
 
@@ -564,18 +579,21 @@
     for o in range(C):
         sg_ref[o] = (coef_rows * back_columns[:, o : o + 1])[:, 0:32]
 
+    lax.fori_loop(0, BX, spread, 0, unroll=4)
     all_of(rzb, 15, zs.at[1], zr.at[1]).wait_recv()
     modes_all = x_z_synthesise(a * 8, rzb, px_ref, zs_ref)
-
-    def last(i):
-        modes = modes_all[128 * i : 128 * i + 128]
-        for y in range(BY):
-            cells = slice(y * NZ, (y + 1) * NZ)
-            oflat[pl.ds(i * BY + y, C, stride=32), :] = acc[i, :, cells] + modes[y * C : (y + 1) * C]
-
-    for i in range(BX):
-        last(i)
-    flatten(oflat, ig_ref)
+    upper = lax.broadcasted_iota(jnp.int32, (128, NZ), 0) % 8 < 4
+    for part in range(2):
+        even, odd = [], []
+        for i in (4 * part, 4 * part + 2):
+            first, second = modes_all[128 * i : 128 * i + 128], modes_all[128 * i + 128 : 128 * i + 256]
+            even.append(jnp.where(upper, first, pltpu.roll(second, 4, 0)))
+            odd.append(jnp.where(upper, pltpu.roll(first, 124, 0), second))
+        for n in range(16):
+            for c, rows in ((2 * n, even), (2 * n + 1, odd)):
+                cells = slice(c * 32 + 16 * part, c * 32 + 16 * part + 16)
+                value = jnp.concatenate([r[8 * n : 8 * n + 8] for r in rows], axis=0) + oflat[cells, :]
+                ig_ref[c, 16 * part : 16 * part + 16, :] = value.astype(bf16)
 
     for n in range(2):
         all_of((rx, rxb)[n], 15, xs.at[n], xr.at[n]).wait_send()
@@ -604,7 +622,9 @@
 
 
 def finish(kr, ig, out, sg, out_hbm, ig_hbm, sg_hbm, kg_hbm, bg_hbm, kg, bg, store_sem):
-    pairs = ((ig, ig_hbm), (out, out_hbm), (sg, sg_hbm), (bg, bg_hbm), (kg, kg_hbm))
+    pairs = ((ig, ig_hbm), (out, out_hbm), (sg, sg_hbm), (bg, bg_hbm)) + tuple(
+        (kg.at[pl.ds(9 * d, 9)], kg_hbm.at[pl.ds(9 * d, 9)]) for d in range(3)
+    )
     stores = [pltpu.make_async_copy(src, dst, store_sem.at[n]) for n, (src, dst) in enumerate(pairs)]
     for store in stores[:3]:
         store.start()
@@ -619,13 +639,13 @@
                     n, offset = (n - 7) * 3 + f, 96
                 moved = blocks[n] if offset == 0 else pltpu.roll(blocks[n], 128 - offset, 1)
                 kg[(d * 3 + e) * 3 + f] = moved[:, 0:32]
-    stores[4].start()
+        stores[4 + d].start()
     for store in stores:
         store.wait()
 
 
 def layer(inputs, cotangent, weights, channel_bias, spectral):
-    z_analysis, z_synthesis, y_table, x_table = tables()
+    z_analysis, z_synthesis, y_table, y_table_back, x_table, scales, y_analysis = tables()
     x = inputs.reshape(C, BX * BY, NZ)
     ct = cotangent.reshape(C, BX * BY, NZ)
     any_space = pl.BlockSpec(memory_space=pl.ANY)
@@ -633,23 +653,24 @@
     dma = pltpu.SemaphoreType.DMA
     V = pltpu.VMEM
     mode_bufs = [
-        V((16, 16, 128), f32), V((16, 16, 128), f32),
+        V((16, 16, 128), bf16), V((16, 16, 128), bf16),
         V((2, 16, 128), bf16), V((16, 2, 16, 128), bf16),
         V((2, 16, 128), bf16), V((16, 16, 128), bf16),
     ]
     block = (C, BX * BY, NZ)
     operands = (
         x, ct, spectral, weights.reshape(27, C, C), channel_bias.reshape(1, C),
-        z_analysis, z_synthesis, y_table, x_table,
+        z_analysis, z_synthesis, y_table, x_table, y_table_back, scales, y_analysis,
     )
     results = pl.pallas_call(
         kernel,
         out_shape=(V(block, bf16), V(block, bf16), V((C, 16, C), f32), V((KG_SHARES, KG_ROWS, 128), bf16)),
-        in_specs=[pl.BlockSpec(memory_space=pltpu.HBM)] * 9,
+        in_specs=[pl.BlockSpec(memory_space=pltpu.HBM)] * 12,
         out_specs=(vmem,) * 4,
         scratch_shapes=[
             V((27, C, C), bf16), V((1, C), f32), V((32, 128), bf16), V((48, 128), bf16),
             V((32, MODES, 128), f32), pltpu.SMEM((NX * MODES,), f32),
+            V((32, MODES, 128), f32), V((48, 128), f32), V((32, MODES, 128), f32), V((2, 128, 128), f32),
             V((C, 1152), bf16), V((C, 1152), bf16), V((C, 128), f32),
             V((C, 32, NZ), bf16), V((C, 32, NZ), bf16), V((C, C, 256), bf16),
             V((C * 32, NZ), f32), V((BX, C, LANES), f32), V((BX, C, LANES), f32),
@@ -663,7 +684,7 @@
             V((KG_ROWS, 128), bf16), V((16, KG_ROWS, 128), bf16),
             V((KG_ROWS, 128), bf16),
             V((C * 32, NZ), f32), V((2, C * C, 128), f32), V((C, C, 256), f32),
-            pltpu.SemaphoreType.REGULAR, dma((11,)), dma((2, 8)), dma((2, 8)),
+            pltpu.SemaphoreType.REGULAR, dma((14,)), dma((2, 8)), dma((2, 8)),
             *[dma((2,))] * 3, dma((2, 4)), *[dma((2,))] * 2,
             *[dma] * 6,
         ],
@@ -687,7 +708,7 @@
         in_specs=[vmem] * 4,
         out_specs=(any_space,) * 5,
         scratch_shapes=[
-            V((27, C, C), f32), V((1, C), f32), dma((5,)),
+            V((27, C, C), f32), V((1, C), f32), dma((7,)),
         ],
         compiler_params=pltpu.CompilerParams(vmem_limit_bytes=16 * 2**20),
     )(shares, input_grad, outputs, spectral_grad)

time: 44.4 us -> 43.9 us (0.989)
  Pallas kernels: 43.7 us -> 43.1 us
    pallas_call x1, Pallas kernels: 42.6 us -> 42 us  [layer(): pl.pallas_call(kernel, out_shape=(V(block, bf16), V(block, bf16), V((C, 1...]
where the time goes in v1:
time: 43.9 us; the launch traced here: 43.8 us
  Pallas kernels  43.1 us (98%)
  between operations  0.64 us (1%)
    pallas_call x1, Pallas kernels, layer(): pl.pallas_call(kernel, out_shape=(V(block, bf16), V(block, bf16), V((C, 1...  42 us
    pallas_call x1, Pallas kernels, layer(): pl.pallas_call(finish, out_shape=(jax.ShapeDtypeStruct(block, bf16), jax....  1.08 us

profile of v1, /device:TPU:1, one launch (start us, length us, event | category | flops | bytes accessed | tf_op | source)
XLA Modules:
  0.0 43.8 jit_solution(16564514367485049932)
XLA Ops:
  0.6 42.0 %shard_map.155 = (bf16[32,32,128]{2,1,0:T(8,128)(2,1)S(1)}, bf16[32,32,128]{2,1,0:T(8,128)(2,1)S(1)}, f32[32,16,32]{2,1,0:T(8,128)S(1)}, bf16[7,32,128]{2,1,0:T(8,128)(2,1)S(1)}) custom-call(bf16[32,32,128]{2,1,0:T(8,128)(2,1)} %bitcast.9, bf16[32,32,128]{2,1,0:T(8,128)(2,1)} %bitcast.10, bf16[32,32,4096]{2,1,0:T(8,128)(2,1)} %spec_hbm.1, ...), custom_call_target="tpu_custom_call" | custom-call | flops 700000000 | bytes 4000000 | tf_op jit(solution)/shard_map/pallas_call | solution.py:665
  42.7 1.1 %shard_map.156 = (bf16[32,32,128]{2,1,0:T(8,128)(2,1)}, bf16[32,32,128]{2,1,0:T(8,128)(2,1)}, f32[32,16,32]{2,1,0:T(8,128)}, f32[27,32,32]{2,1,0:T(8,128)}, f32[1,32]{1,0:T(1,128)}) custom-call(bf16[7,32,128]{2,1,0:T(8,128)(2,1)S(1)} %get-tuple-element.14.kr, bf16[32,32,128]{2,1,0:T(8,128)(2,1)S(1)} %get-tuple-element.15.ig, ...), custom_call_target="tpu_custom_call" | custom-call | tf_op jit(solution)/shard_map/pallas_call | solution.py:699

commit v2 on v1

--- a/solution.py
+++ b/solution.py
@@ -287,7 +287,7 @@
         for n in range(2):
             for j in range(BY):
                 wide_ref[n, pl.ds(j, C, stride=BY), :] = modes[:, 128 * n : 128 * n + 128] * scale
-        tall = jnp.concatenate([jnp.transpose(wide_ref[n]) for n in range(2)], axis=0)
+        tall = jnp.concatenate([jnp.transpose(wide_ref[n, 0:128, :]) for n in range(2)], axis=0)
         y_project(tall, pb_ref, send)
 
     def y_project(tall, table, send):
@@ -670,10 +670,10 @@
         scratch_shapes=[
             V((27, C, C), bf16), V((1, C), f32), V((32, 128), bf16), V((48, 128), bf16),
             V((32, MODES, 128), f32), pltpu.SMEM((NX * MODES,), f32),
-            V((32, MODES, 128), f32), V((48, 128), f32), V((32, MODES, 128), f32), V((2, 128, 128), f32),
+            V((32, MODES, 128), f32), V((48, 128), f32), V((32, MODES, 128), f32), V((2, 136, 128), f32),
             V((C, 1152), bf16), V((C, 1152), bf16), V((C, 128), f32),
             V((C, 32, NZ), bf16), V((C, 32, NZ), bf16), V((C, C, 256), bf16),
-            V((C * 32, NZ), f32), V((BX, C, LANES), f32), V((BX, C, LANES), f32),
+            V((C * 32 + 32, NZ), f32), V((BX, C, LANES), f32), V((BX, C, LANES), f32),
             V((10, 128, WIDE), bf16), V((10, 128, WIDE), bf16), V((12, C, LANES), bf16),
             V((BX, 16, 128), f32),
             *mode_bufs,
@@ -683,7 +683,7 @@
             V((KG_SHARES, KG_ROWS, 128), bf16), V((16, KG_ROWS, 128), bf16),
             V((KG_ROWS, 128), bf16), V((16, KG_ROWS, 128), bf16),
             V((KG_ROWS, 128), bf16),
-            V((C * 32, NZ), f32), V((2, C * C, 128), f32), V((C, C, 256), f32),
+            V((C * 32 + 32, NZ), f32), V((2, C * C + 32, 128), f32), V((C, C, 256), f32),
             pltpu.SemaphoreType.REGULAR, dma((14,)), dma((2, 8)), dma((2, 8)),
             *[dma((2,))] * 3, dma((2, 4)), *[dma((2,))] * 2,
             *[dma] * 6,

time: 43.9 us -> 43.9 us (level)
  no operation moved by 1% of the time
where the time goes in v2:
time: 43.9 us; the launch traced here: 43.8 us
  Pallas kernels  43.1 us (98%)
  between operations  0.64 us (1%)
    pallas_call x1, Pallas kernels, layer(): pl.pallas_call(kernel, out_shape=(V(block, bf16), V(block, bf16), V((C, 1...  42 us
    pallas_call x1, Pallas kernels, layer(): pl.pallas_call(finish, out_shape=(jax.ShapeDtypeStruct(block, bf16), jax....  1.08 us

profile of v2, /device:TPU:1, one launch (start us, length us, event | category | flops | bytes accessed | tf_op | source)
XLA Modules:
  0.0 43.8 jit_solution(2367423293714646561)
XLA Ops:
  0.6 42.0 %shard_map.155 = (bf16[32,32,128]{2,1,0:T(8,128)(2,1)S(1)}, bf16[32,32,128]{2,1,0:T(8,128)(2,1)S(1)}, f32[32,16,32]{2,1,0:T(8,128)S(1)}, bf16[7,32,128]{2,1,0:T(8,128)(2,1)S(1)}) custom-call(bf16[32,32,128]{2,1,0:T(8,128)(2,1)} %bitcast.9, bf16[32,32,128]{2,1,0:T(8,128)(2,1)} %bitcast.10, bf16[32,32,4096]{2,1,0:T(8,128)(2,1)} %spec_hbm.1, ...), custom_call_target="tpu_custom_call" | custom-call | flops 700000000 | bytes 4000000 | tf_op jit(solution)/shard_map/pallas_call | solution.py:665
  42.7 1.1 %shard_map.156 = (bf16[32,32,128]{2,1,0:T(8,128)(2,1)}, bf16[32,32,128]{2,1,0:T(8,128)(2,1)}, f32[32,16,32]{2,1,0:T(8,128)}, f32[27,32,32]{2,1,0:T(8,128)}, f32[1,32]{1,0:T(1,128)}) custom-call(bf16[7,32,128]{2,1,0:T(8,128)(2,1)S(1)} %get-tuple-element.14.kr, bf16[32,32,128]{2,1,0:T(8,128)(2,1)S(1)} %get-tuple-element.15.ig, ...), custom_call_target="tpu_custom_call" | custom-call | tf_op jit(solution)/shard_map/pallas_call | solution.py:699
